TPU v7x, 256 devices: a whole 4x4x8 slice. The times are simulated.
256 devices in a mesh: pipe: 8 (over z_hi, x), dp: 4 (over y), tensor: 8 (over z_lo, core).
Axes of the slice: x: 4, y: 4, z: 8 (z_hi: 2, z_lo: 4; z = z_hi * 4 + z_lo), core: 2. Of those that a mesh axis runs over, the one named last changes fastest.
Arguments:
- enc_states: bfloat16 [4, 128, 8192], P('dp', None, ('pipe', 'tensor')), may hold values from -6 to 6
- enc_len: int32 [4], P('dp'), may hold values from 64 to 128
- queries: bfloat16 [8, 4, 256, 8192], P('pipe', 'dp', None, 'tensor'), may hold values from -500 to 500
- kv_weight: bfloat16 [8, 8192, 2, 8192], P('pipe', 'dp', None, 'tensor'), may hold values from -0.0625 to 0.0625
- ctx_grad: bfloat16 [8, 4, 256, 8192], P('pipe', 'dp', None, 'tensor'), may hold values from -24 to 24
Outputs:
- context: bfloat16 [8, 4, 256, 8192], P('pipe', 'dp', None, 'tensor')
- enc_grad: float32 [4, 128, 8192], P('dp', None, ('pipe', 'tensor'))
All inputs are finite; a program needn't handle non-finite values.
Results may differ from a plain program's by a relative error of at most 0.014.
Values may be sent and summed in bfloat16 or wider, within the bound.
A program may use at most 192 MiB of HBM per device.

v0:
```python
import math

import jax
import jax.numpy as jnp
from jax import lax
from jax.sharding import PartitionSpec as P

HEAD_DIM = 128


def on_device(enc_states, enc_len, queries, kv_weight, ctx_grad):
    gathered = lax.all_gather(kv_weight, "dp", axis=1, tiled=True)
    head_cols = gathered.shape[3]
    width = gathered.shape[1]
    flat_weight = gathered[0].reshape(width, 2 * head_cols)
    own_cols = enc_states[0]
    enc_rows = own_cols.shape[0]
    cols_dev = own_cols.shape[1]
    highest = lax.Precision.HIGHEST
    weight_rows = flat_weight
    keys_values = jnp.dot(
        lax.all_gather(own_cols, ("pipe", "tensor"), axis=1, tiled=True),
        weight_rows,
        preferred_element_type=jnp.float32,
    )
    dec_rows = queries.shape[2]
    heads_here = head_cols // HEAD_DIM
    factor = 1.0 / math.sqrt(HEAD_DIM)
    keys_part = keys_values[:, :head_cols].reshape(enc_rows, heads_here, HEAD_DIM)
    values_part = keys_values[:, head_cols:].reshape(enc_rows, heads_here, HEAD_DIM)
    query_heads = queries[0, 0].reshape(dec_rows, heads_here, HEAD_DIM)
    grad_heads = ctx_grad[0, 0].reshape(dec_rows, heads_here, HEAD_DIM)
    scores = (
        jnp.einsum("qhd,khd->hqk", query_heads.astype(jnp.float32), keys_part, precision=highest)
        * factor
    )
    live_keys = jnp.arange(enc_rows, dtype=jnp.int32) < enc_len[0]
    scores = jnp.where(live_keys[None, None, :], scores, -1e30)
    top_score = jnp.max(scores, axis=-1, keepdims=True)
    expd = jnp.exp(scores - top_score)
    probs_all = expd / jnp.sum(expd, axis=-1, keepdims=True)
    attn_bf = probs_all.astype(jnp.bfloat16)
    context = jnp.einsum(
        "hqk,khd->qhd", attn_bf.astype(jnp.float32), values_part, precision=highest
    )
    context = context.reshape(1, 1, dec_rows, head_cols).astype(jnp.bfloat16)
    probs_grad = jnp.einsum(
        "qhd,khd->hqk", grad_heads.astype(jnp.float32), values_part, precision=highest
    )
    row_dots = jnp.sum(probs_all * probs_grad, axis=-1, keepdims=True)
    score_grad = (probs_all * (probs_grad - row_dots) * factor).astype(jnp.bfloat16)
    key_grad = jnp.einsum(
        "hqk,qhd->khd", score_grad, query_heads, preferred_element_type=jnp.float32
    )
    value_grad = jnp.einsum("hqk,qhd->khd", attn_bf, grad_heads, preferred_element_type=jnp.float32)
    kv_grad = jnp.concatenate(
        [key_grad.reshape(enc_rows, head_cols), value_grad.reshape(enc_rows, head_cols)], axis=1
    ).astype(jnp.bfloat16)
    weight_rows = flat_weight
    enc_part = lax.psum_scatter(
        lax.dot_general(
            weight_rows, kv_grad, (((1,), (1,)), ((), ())), preferred_element_type=jnp.float32
        ),
        ("pipe", "tensor"),
        scatter_dimension=0,
        tiled=True,
    )
    return (context, enc_part.T.reshape(1, enc_rows, cols_dev))


def solution(mesh):
    return jax.shard_map(
        on_device,
        mesh=mesh,
        in_specs=(
            P("dp", None, ("pipe", "tensor")),
            P("dp"),
            P("pipe", "dp", None, "tensor"),
            P("pipe", "dp", None, "tensor"),
            P("pipe", "dp", None, "tensor"),
        ),
        out_specs=(P("pipe", "dp", None, "tensor"), P("dp", None, ("pipe", "tensor"))),
        check_vma=False,
    )
```

profile of v0, /device:TPU:16, one launch (start us, length us, event | category | flops | bytes accessed | tf_op | source)
XLA Modules:
  0.0 731.6 jit_solution(17756325723849344305)
XLA Ops:
  7.2 0.0 all-gather.4.cloned.1.call-start
  7.2 0.7 all-gather.4.cloned.1.call-update
  7.9 0.0 all-gather.6.cloned.1.call-start
  7.9 0.7 all-gather.6.cloned.1.call-update
  8.6 0.0 reduce-scatter.2.cloned.1.call-start
  8.7 1.2 copy.33
  10.6 1.2 copy.34
  11.9 296.9 %all-gather.4.cloned.1.call-done = bf16[1,8192,2,1024]{3,2,0,1:T(2,128)(2,1)} async-done(((bf16[1,2048,2,1024]{3,2,0,1:T(2,128)(2,1)}), bf16[1,8192,2,1024]{3,2,0,1:T(2,128)(2,1)}) %all-gather.4.cloned.1.call-update) | async-done | bytes 33554448 | tf_op jit(solution)/shard_map/all_gather | solution.py:12
  308.8 23.3 %copy.37 = bf16[1024,8,2,1024]{3,1,2,0:T(8,128)(2,1)} copy(bf16[1024,8,2,1024]{3,2,1,0:T(2,128)(2,1)} %bitcast.52) | data formatting | bytes 67108864
  332.1 91.5 %all-gather.6.cloned.1.call-done = bf16[1,128,8192]{2,1,0:T(8,128)(2,1)} async-done(((bf16[1,128,128]{2,1,0:T(8,128)(2,1)}), bf16[1,128,8192]{2,1,0:T(8,128)(2,1)}) %all-gather.6.cloned.1.call-update) | async-done | bytes 2097168 | tf_op jit(solution)/shard_map/all_gather | solution.py:22
  423.5 13.5 %fusion.2 = f32[128,2048]{1,0:T(8,128)S(1)} fusion(bf16[8192,2048]{1,0:T(8,128)(2,1)} %bitcast.50, bf16[1,128,8192]{2,1,0:T(8,128)(2,1)} %all-gather.6.cloned.1.call-done), kind=kOutput, calls=%fused_computation.3 | convolution fusion | flops 4294967296 | bytes 36700160 | tf_op jit(solution)/shard_map/dot_general | solution.py:21
  437.0 0.1 slice_bitcast_fusion
  437.1 0.6 fusion.10
  437.7 1.2 fusion.31
  438.9 1.5 convolution_bitcast_fusion.1
  440.5 0.4 convolution_convert_fusion.1
  440.9 0.0 copy-start
  440.9 2.8 fusion.13
  443.7 18.5 %convolution_bitcast_fusion = f32[8192,128]{0,1:T(8,128)} fusion(bf16[8192,2048]{1,0:T(8,128)(2,1)} %bitcast.51, bf16[128,1024]{0,1:T(8,128)(2,1)S(1)} %bitcast.59, bf16[128,1024]{0,1:T(8,128)(2,1)S(1)} %bitcast.60), kind=kOutput, calls=%fused_computation.2 | convolution fusion | flops 4296015872 | bytes 38273024 | tf_op jit(solution)/shard_map/dot_general | solution.py:61
  462.1 0.0 reduce-scatter.2.cloned.1.call-update
  462.2 0.0 copy-done
  462.2 0.6 convolution_convert_fusion
  462.8 1.0 copy.29
  463.8 261.3 %reduce-scatter.2.cloned.1.call-done = f32[128,128]{0,1:T(8,128)} async-done(((f32[8192,128]{0,1:T(8,128)}), f32[128,128]{0,1:T(8,128)}) %reduce-scatter.2.cloned.1.call-update) | async-done | bytes 65552 | tf_op jit(solution)/shard_map/reduce_scatter | solution.py:60
  (1 shorter events, 0.0 us)
Async XLA Ops:
  7.2 301.6 %all-gather.4.cloned.1.call-start = ((), (), s32[]{:S(2)}) async-start(), calls=%async_computation.1 | async-start | bytes 41943040 | tf_op jit(solution)/shard_map/all_gather | solution.py:12
  7.9 415.6 %all-gather.6.cloned.1.call-start = ((), (), s32[]{:S(2)}) async-start(), calls=%async_computation.3 | async-start | bytes 2129920 | tf_op jit(solution)/shard_map/all_gather | solution.py:22
  8.6 716.4 %reduce-scatter.2.cloned.1.call-start = ((), (), s32[]{:S(2)}) async-start(), calls=%async_computation.2 | async-start | bytes 4259840 | tf_op jit(solution)/shard_map/reduce_scatter | solution.py:60
  440.9 21.3 %copy-start = (f32[8,256,128]{1,2,0:T(8,128)S(1)}, f32[8,256,128]{1,2,0:T(8,128)}, u32[]{:S(2)}) copy-start(f32[8,256,128]{1,2,0:T(8,128)} %get-tuple-element.9) | copy-start | bytes 3145732
Sparse Core Ops, SparseCore 0:
  9.8 298.9 all-gather.3
  310.6 112.9 all-gather.5
  462.3 262.7 reduce-scatter.1
where the time goes:
time: 732 us
  waiting for transfers between devices  651 us (89%)
  matrix products  37.9 us (5%)
  local copies, waits for them, and re-layouts  26.9 us (4%)
  between operations  14.5 us (2%)
    all_gather x1, waiting for transfers between devices, on_device(): gathered = lax.all_gather(kv_weight, 'dp', axis=1, tiled=True)  297 us
    reduce_scatter x1, waiting for transfers between devices, on_device(): lax.psum_scatter(lax.dot_general(weight_rows, kv_grad, (((1,), (1,)), (()...  261 us
    all_gather x1, waiting for transfers between devices, on_device(): lax.all_gather(own_cols, ('pipe', 'tensor'), axis=1, tiled=True)  91.5 us
    unnamed x5, local copies, waits for them, and re-layouts  24.4 us
    dot_general x1, matrix products, on_device(): lax.dot_general(weight_rows, kv_grad, (((1,), (1,)), ((), ())), preferred...  18.5 us
  transfers between devices with their start and end apart: 3, of which 3 were waited for; matrix products, arithmetic and copies ran while one was open for 4% of the time, Pallas kernels for 0%

commit v1 on v0

v1 whole, which is shorter than its diff:
```python
import math

import jax
import jax.numpy as jnp
from jax import lax
from jax.experimental import pallas as pl
from jax.experimental.pallas import tpu as pltpu
from jax.sharding import PartitionSpec as P

HEAD_DIM = 128
TOK = 128
FB = 128
HEADS_HERE = 8
COLS = HEADS_HERE * HEAD_DIM
DEC = 256
ROWS = 2048
HALF = ROWS // 2
BF = jnp.bfloat16
F32 = jnp.float32
MESH = pl.DeviceIdType.MESH


def dot(a, b, dims):
    return lax.dot_general(a, b, (dims, ((), ())), preferred_element_type=F32)


def kernel(
    x_ref, len_ref, q_hbm, w_hbm, g_hbm, ctx_hbm, out_ref,
    states, w, q, g, kb, vb, kr, vr, kvg, ctx, po, ps, pr, s2, r2, tot, s3, r3, s4, r4,
    w_sem, in_sem, a1s, a1r, a2s, a2r, a3s, a3r, a4s, a4r,
    bks, bkr, bvs, bvr, cs, cr, e1s, e1r, e2s, e2r, e3s, e3r, e4s, e4r,
):
    p = lax.axis_index("pipe")
    y = lax.axis_index("dp")
    t = lax.axis_index("tensor")
    zh, x = p // 4, p % 4
    zl, core = t // 2, t % 2
    z = zh * 4 + zl

    def at(x_, y_, z_, core_):
        return ((z_ // 4) * 4 + x_, y_, (z_ % 4) * 2 + core_)

    def remote(src, dst, send, recv, dev):
        return pltpu.make_async_remote_copy(
            src_ref=src, dst_ref=dst, send_sem=send, recv_sem=recv,
            device_id=dev, device_id_type=MESH,
        )

    def lanes(index, size):
        return pl.ds(pl.multiple_of(index * size, size), size)

    zs = [at(x, y, (z + k) % 8, core) for k in range(8)]
    xs = [at((x + k) % 4, y, z, core) for k in range(4)]
    ys = [at(x, (y + k) % 4, z, core) for k in range(4)]
    sibling = at(x, y, z, 1 - core)
    hold_z = (1 - p % 2) * 4 + zl
    holder = at(y, p // 2, hold_z, core)
    owner = (2 * y + (1 - zh), x, t)

    loads = []
    for place in range(16):
        c_, z_ = place // 8, place % 8
        block = (1 - z_ // 4) * 8 + (z_ % 4) * 2 + c_
        loads.append(
            pltpu.make_async_copy(
                w_hbm.at[pl.ds(block * FB, FB)], w.at[pl.ds(place * FB, FB)], w_sem.at[place]
            )
        )
    load_q = pltpu.make_async_copy(q_hbm, q, in_sem.at[0])
    load_g = pltpu.make_async_copy(g_hbm, g, in_sem.at[1])
    for load in loads + [load_q, load_g]:
        load.start()

    barrier = pltpu.get_barrier_semaphore()
    partners = zs[1:] + xs[1:] + ys[1:] + [sibling, holder, owner]
    for dev in partners:
        pl.semaphore_signal(barrier, inc=1, device_id=dev, device_id_type=MESH)
    pl.semaphore_wait(barrier, len(partners))

    first = remote(
        x_ref, states.at[y, :, lanes(core * 8 + hold_z, FB)], a1s.at[0], a1r.at[0], holder
    )
    first.start()
    mine = states.at[x, :, lanes(core * 8 + z, FB)]
    remote(x_ref, mine, a1s.at[0], a1r.at[0], holder).wait_recv()
    along_z = [remote(mine, mine, a2s.at[k - 1], a2r.at[k - 1], zs[k]) for k in range(1, 8)]
    for copy in along_z:
        copy.start()
    for k in range(1, 8):
        theirs = states.at[x, :, lanes(core * 8 + (z + 8 - k) % 8, FB)]
        remote(theirs, theirs, a2s.at[k - 1], a2r.at[k - 1], zs[k]).wait_recv()
    row = states.at[x, :, lanes(core, HALF)]
    along_x = [remote(row, row, a3s.at[k - 1], a3r.at[k - 1], xs[k]) for k in range(1, 4)]
    for copy in along_x:
        copy.start()
    across = []
    for k in range(4):
        seq = (x + 4 - k) % 4
        row = states.at[seq, :, lanes(core, HALF)]
        if k:
            remote(row, row, a3s.at[k - 1], a3r.at[k - 1], xs[k]).wait_recv()
        across.append(remote(row, row, a4s.at[k], a4r.at[k], sibling))
        across[-1].start()
    for k in range(4):
        row = states.at[(x + 4 - k) % 4, :, lanes(1 - core, HALF)]
        remote(row, row, a4s.at[k], a4r.at[k], sibling).wait_recv()
    for load in loads:
        load.wait()

    def project(c, _):
        cols = lanes(c, 256)
        vcols = pl.ds(pl.multiple_of(COLS + c * 256, 256), 256)
        lhs = states[...].reshape(4 * TOK, ROWS)
        kb[:, :, cols] = dot(lhs, w[:, cols], ((1,), (0,))).reshape(4, TOK, 256)
        vb[:, :, cols] = dot(lhs, w[:, vcols], ((1,), (0,))).reshape(4, TOK, 256).astype(BF)
        return 0

    lax.fori_loop(0, COLS // 256, project, 0)

    key_copies, value_copies = {}, {}
    for k in (2, 1, 3):
        seq = (y + k) % 4
        key_copies[k] = remote(kb.at[seq], kr.at[k - 1], bks.at[k - 1], bkr.at[k - 1], ys[k])
        value_copies[k] = remote(vb.at[seq], vr.at[k - 1], bvs.at[k - 1], bvr.at[k - 1], ys[k])
        key_copies[k].start()
        value_copies[k].start()
    load_q.wait()
    load_g.wait()
    for k in (1, 3, 2):
        key_copies[k].wait_recv()
        value_copies[k].wait_recv()

    factor = 1.0 / math.sqrt(HEAD_DIM)
    live = lax.broadcasted_iota(jnp.int32, (TOK, DEC), 0) < len_ref[0]

    def one_head(h):
        cols = lanes(h, HEAD_DIM)
        vcols = pl.ds(pl.multiple_of(COLS + h * HEAD_DIM, HEAD_DIM), HEAD_DIM)
        keys = kb[y, :, cols] + kr[0, :, cols] + kr[1, :, cols] + kr[2, :, cols]
        values = (
            vb[y, :, cols].astype(F32) + vr[0, :, cols].astype(F32)
            + vr[1, :, cols].astype(F32) + vr[2, :, cols].astype(F32)
        )
        k1 = keys.astype(BF)
        rest = keys - k1.astype(F32)
        k2 = rest.astype(BF)
        k3 = (rest - k2.astype(F32)).astype(BF)
        v1 = values.astype(BF)
        v2 = (values - v1.astype(F32)).astype(BF)
        qh, gh = q[:, cols], g[:, cols]
        nt, nn, tn = ((1,), (1,)), ((1,), (0,)), ((0,), (0,))
        scores = (dot(k3, qh, nt) + dot(k2, qh, nt) + dot(k1, qh, nt)) * factor
        scores = jnp.where(live, scores, -1e30)
        top = jnp.max(scores, axis=0, keepdims=True)
        expd = jnp.exp(scores - top)
        probs = expd / jnp.sum(expd, axis=0, keepdims=True)
        attn = probs.astype(BF)
        ctx[:, cols] = (dot(attn, v2, tn) + dot(attn, v1, tn)).astype(BF)
        probs_grad = dot(v2, gh, nt) + dot(v1, gh, nt)
        row_dots = jnp.sum(probs * probs_grad, axis=0, keepdims=True)
        score_grad = (probs * (probs_grad - row_dots) * factor).astype(BF)
        kvg[0, :, cols] = dot(score_grad, qh, nn).astype(BF)
        kvg[0, :, vcols] = dot(attn, gh, nn).astype(BF)

    def two_heads(i, _):
        one_head(2 * i)
        one_head(2 * i + 1)
        return 0

    lax.fori_loop(0, HEADS_HERE // 2, two_heads, 0)

    save_ctx = pltpu.make_async_copy(ctx, ctx_hbm, in_sem.at[2])
    save_ctx.start()
    grad_copies = {}
    for k in (2, 1, 3):
        grad_copies[k] = remote(kvg.at[0], kvg.at[4 - k], cs.at[k - 1], cr.at[k - 1], ys[k])
        grad_copies[k].start()
    for k in (1, 3, 2):
        back = kvg.at[4 - k]
        remote(back, back, cs.at[k - 1], cr.at[k - 1], ys[k]).wait_recv()

    def terms(half, i):
        rows = pl.ds(pl.multiple_of(half * HALF + i * 256, 256), 256)
        return dot(w[rows, :], kvg[...].reshape(4 * TOK, 2 * COLS), ((1,), (1,)))

    def give(i):
        return remote(
            ps.at[:, pl.ds(i * 256, 256)], pr.at[:, pl.ds(i * 256, 256)],
            e1s.at[i], e1r.at[i], sibling,
        )

    for i in range(4):
        acc = terms(1 - core, i)
        for k in range(4):
            ps[(y + k) % 4, pl.ds(i * 256, 256), :] = acc[:, k * TOK:(k + 1) * TOK].astype(BF)
        give(i).start()
    for i in range(4):
        acc = terms(core, i)
        for k in range(4):
            po[(y + k) % 4, pl.ds(i * 256, 256), :] = acc[:, k * TOK:(k + 1) * TOK]
    for i in range(4):
        give(i).wait_recv()

    out_x = [remote(s2.at[k], r2.at[k], e2s.at[k], e2r.at[k], xs[k + 1]) for k in range(3)]
    for k in (1, 0, 2):
        seq = (x + k + 1) % 4
        s2[k] = (po[seq] + pr[seq].astype(F32)).astype(BF)
        out_x[k].start()
    tot[...] = (po[x] + pr[x].astype(F32)).reshape(8, FB, TOK)
    for k in (0, 2, 1):
        out_x[k].wait_recv()
        tot[...] += r2[k].astype(F32).reshape(8, FB, TOK)
    out_z = []
    for k in (4, 3, 5, 2, 6, 1, 7):
        s3[k - 1] = tot[(z + k) % 8].astype(BF)
        out_z.append(remote(s3.at[k - 1], r3.at[k - 1], e3s.at[k - 1], e3r.at[k - 1], zs[k]))
        out_z[-1].start()
    for copy in out_z:
        copy.wait_recv()
    total = tot[z]
    for k in range(7):
        total += r3[k].astype(F32)
    s4[...] = total.T
    last = remote(s4, r4, e4s.at[0], e4r.at[0], owner)
    last.start()
    last.wait_recv()
    out_ref[...] = r4[...]

    save_ctx.wait()
    first.wait_send()
    last.wait_send()
    for copy in along_z + along_x + across + out_x + out_z:
        copy.wait_send()
    for k in (1, 2, 3):
        key_copies[k].wait_send()
        value_copies[k].wait_send()
        grad_copies[k].wait_send()
    for i in range(4):
        give(i).wait_send()


def on_device(enc_states, enc_len, queries, kv_weight, ctx_grad):
    any_spec = pl.BlockSpec(memory_space=pl.ANY)
    vmem = pltpu.VMEM
    dma = lambda n: pltpu.SemaphoreType.DMA((n,))
    context, enc_grad = pl.pallas_call(
        kernel,
        out_shape=(
            jax.ShapeDtypeStruct((DEC, COLS), BF),
            jax.ShapeDtypeStruct((TOK, FB), F32),
        ),
        in_specs=[any_spec, pl.BlockSpec(memory_space=pltpu.SMEM)] + [any_spec] * 3,
        out_specs=(any_spec, pl.BlockSpec(memory_space=pltpu.VMEM)),
        scratch_shapes=[
            vmem((4, TOK, ROWS), BF),
            vmem((ROWS, 2 * COLS), BF),
            vmem((DEC, COLS), BF),
            vmem((DEC, COLS), BF),
            vmem((4, TOK, COLS), F32),
            vmem((4, TOK, COLS), BF),
            vmem((3, TOK, COLS), F32),
            vmem((3, TOK, COLS), BF),
            vmem((4, TOK, 2 * COLS), BF),
            vmem((DEC, COLS), BF),
            vmem((4, HALF, TOK), F32),
            vmem((4, HALF, TOK), BF),
            vmem((4, HALF, TOK), BF),
            vmem((3, HALF, TOK), BF),
            vmem((3, HALF, TOK), BF),
            vmem((8, FB, TOK), F32),
            vmem((7, FB, TOK), BF),
            vmem((7, FB, TOK), BF),
            vmem((TOK, FB), F32),
            vmem((TOK, FB), F32),
            dma(16), dma(3), dma(1), dma(1), dma(7), dma(7), dma(3), dma(3), dma(4), dma(4),
            dma(3), dma(3), dma(3), dma(3), dma(3), dma(3), dma(4), dma(4),
            dma(3), dma(3), dma(7), dma(7), dma(1), dma(1),
        ],
        compiler_params=pltpu.CompilerParams(
            collective_id=0, has_side_effects=True, vmem_limit_bytes=50 * 2**20
        ),
    )(
        enc_states[0],
        enc_len,
        queries[0, 0],
        kv_weight[0].reshape(ROWS, 2 * COLS),
        ctx_grad[0, 0],
    )
    return (context[None, None], enc_grad[None])


def solution(mesh):
    return jax.shard_map(
        on_device,
        mesh=mesh,
        in_specs=(
            P("dp", None, ("pipe", "tensor")),
            P("dp"),
            P("pipe", "dp", None, "tensor"),
            P("pipe", "dp", None, "tensor"),
            P("pipe", "dp", None, "tensor"),
        ),
        out_specs=(P("pipe", "dp", None, "tensor"), P("dp", None, ("pipe", "tensor"))),
        check_vma=False,
    )
```

time: 732 us -> 156 us (0.21)
  waiting for transfers between devices: 651 us -> 0 us
  Pallas kernels: 0 us -> 142 us
  matrix products: 37.9 us -> 0 us
  local copies, waits for them, and re-layouts: 26.9 us -> 11.7 us
  between operations: 14.5 us -> 1.31 us
    all_gather x2 -> x0, waiting for transfers between devices: 388 us -> none  [the longest x1 297 us: on_device(): gathered = lax.all_gather(kv_weight, 'dp', axis=1, tiled=True)]
    reduce_scatter x1 -> x0, waiting for transfers between devices: 261 us -> none  [on_device(): lax.psum_scatter(lax.dot_general(weight_rows, kv_grad, (((1,), (1,)), (()...]
    pallas_call x0 -> x1, Pallas kernels: none -> 142 us  [on_device(): pl.pallas_call(kernel, out_shape=(jax.ShapeDtypeStruct((DEC, COLS), BF),...]
    dot_general x7 -> x0, matrix products: 37.9 us -> none  [the longest x1 18.5 us: on_device(): lax.dot_general(weight_rows, kv_grad, (((1,), (1,)), ((), ())), preferred...]
    unnamed x5 -> x9, local copies, waits for them, and re-layouts: 24.4 us -> 11.7 us
  transfers between devices with their start and end apart: 3 -> 0, of which waited for: 3 -> 0; matrix products, arithmetic and copies ran while one was open for 4% -> 0% of each run, Pallas kernels for 0% -> 0%
where the time goes in v1:
time: 156 us; the launch traced here: 155 us
  Pallas kernels  142 us (91%)
  local copies, waits for them, and re-layouts  11.7 us (8%)
    pallas_call x1, Pallas kernels, on_device(): pl.pallas_call(kernel, out_shape=(jax.ShapeDtypeStruct((DEC, COLS), BF),...  142 us
    unnamed x9, local copies, waits for them, and re-layouts  11.7 us

profile of v1, /device:TPU:16, one launch (start us, length us, event | category | flops | bytes accessed | tf_op | source)
XLA Modules:
  0.0 155.2 jit_solution(7341396749924689695)
XLA Ops:
  1.3 0.0 copy-start
  1.3 0.0 copy-start.1
  1.3 0.0 copy-start.2
  1.3 10.2 %copy.7 = bf16[256,8,2,1024]{3,1,2,0:T(8,128)(2,1)} copy(bf16[256,8,2,1024]{3,2,1,0:T(2,128)(2,1)} %bitcast.14) | data formatting | bytes 16777216
  11.5 0.0 copy-done
  11.5 0.0 copy-done.1
  11.5 0.0 copy-done.2
  11.5 142.2 %shard_map.68 = (bf16[256,1024]{1,0:T(8,128)(2,1)S(1)}, f32[128,128]{1,0:T(8,128)S(1)}) custom-call(bf16[128,128]{1,0:T(8,128)(2,1)S(1)} %bitcast.12, s32[1]{0:T(128)S(6)} %copy.10.len_ref, bf16[256,1024]{1,0:T(8,128)(2,1)S(1)} %bitcast.8, bf16[2048,2048]{1,0:T(8,128)(2,1)} %bitcast.13, bf16[256,1024]{1,0:T(8,128)(2,1)S(1)} %bitcast.9), custom_call_target="tpu_custom_call" | custom-call | tf_op jit(solution)/shard_map/pallas_call | solution.py:246
  153.7 0.8 copy.11
  154.5 0.6 copy.12
Async XLA Ops:
  1.3 10.2 %copy-start = (bf16[1,1,256,1024]{3,2,1,0:T(8,128)(2,1)S(1)}, bf16[1,1,256,1024]{3,2,1,0:T(8,128)(2,1)}, u32[]{:S(2)}) copy-start(bf16[1,1,256,1024]{3,2,1,0:T(8,128)(2,1)} %param.7) | copy-start | bytes 1572868
  1.3 10.2 %copy-start.1 = (bf16[1,1,256,1024]{3,2,1,0:T(8,128)(2,1)S(1)}, bf16[1,1,256,1024]{3,2,1,0:T(8,128)(2,1)}, u32[]{:S(2)}) copy-start(bf16[1,1,256,1024]{3,2,1,0:T(8,128)(2,1)} %param.9) | copy-start | bytes 1572868
  1.3 10.2 %copy-start.2 = (bf16[1,128,128]{2,1,0:T(8,128)(2,1)S(1)}, bf16[1,128,128]{2,1,0:T(8,128)(2,1)}, u32[]{:S(2)}) copy-start(bf16[1,128,128]{2,1,0:T(8,128)(2,1)} %param.5) | copy-start | bytes 98308

commit v2 on v1

v2 whole, which is shorter than its diff:
```python
import math

import jax
import jax.numpy as jnp
from jax import lax
from jax.experimental import pallas as pl
from jax.experimental.pallas import tpu as pltpu
from jax.sharding import PartitionSpec as P

HEAD_DIM = 128
TOK = 128
FB = 128
HEADS_HERE = 8
GROUPS = 4
COLS = HEADS_HERE * HEAD_DIM
DEC = 256
ROWS = 2048
HALF = ROWS // 2
BF = jnp.bfloat16
F32 = jnp.float32
MESH = pl.DeviceIdType.MESH


def dot(a, b, dims):
    return lax.dot_general(a, b, (dims, ((), ())), preferred_element_type=F32)


def kernel(
    x_ref, len_ref, q_hbm, w_hbm, g_hbm, ctx_hbm, out_ref,
    states, wv, w, q, g, kb, vb, mk, mv, fk, fv, kr, vr, kvg, ctx,
    po, ps, pr, s2, r2, tot, s3, r3, mine, s4, r4,
    in_sem, a1s, a1r, a2s, a2r, a3s, a3r, a4s, a4r,
    bs, br, cs, cr, e1s, e1r, e2s, e2r, e3s, e3r, e4s, e4r,
):
    p = lax.axis_index("pipe")
    y = lax.axis_index("dp")
    t = lax.axis_index("tensor")
    zh, x = p // 4, p % 4
    zl, core = t // 2, t % 2
    z = zh * 4 + zl

    def at(x_, y_, z_, core_):
        return ((z_ // 4) * 4 + x_, y_, (z_ % 4) * 2 + core_)

    sent = []

    def remote(src, dst, send, recv, dev):
        return pltpu.make_async_remote_copy(
            src_ref=src, dst_ref=dst, send_sem=send, recv_sem=recv,
            device_id=dev, device_id_type=MESH,
        )

    def post(src, dst, send, recv, dev):
        copy = remote(src, dst, send, recv, dev)
        copy.start()
        sent.append(copy)

    def arrived(dst, send, recv):
        remote(dst, dst, send, recv, sibling).wait_recv()

    def part(index, size):
        return pl.ds(pl.multiple_of(index * size, size), size)

    zs = [at(x, y, (z + k) % 8, core) for k in range(8)]
    xs = [at((x + k) % 4, y, z, core) for k in range(4)]
    right, left = at(x, (y + 1) % 4, z, core), at(x, (y + 3) % 4, z, core)
    sibling = at(x, y, z, 1 - core)
    hold_x, hold_z = zl, 2 * y + 1 - p % 2
    holder = at(hold_x, p // 2, hold_z, core)
    owner = (2 * y + 1 - z % 2, z // 2, x * 2 + core)

    load_w = pltpu.make_async_copy(w_hbm, wv, in_sem.at[0])
    load_q = pltpu.make_async_copy(q_hbm, q, in_sem.at[1])
    load_g = pltpu.make_async_copy(g_hbm, g, in_sem.at[2])
    for load in (load_w, load_q, load_g):
        load.start()

    barrier = pltpu.get_barrier_semaphore()
    partners = zs[1:] + xs[1:] + [right, left, sibling, holder, owner]
    for dev in partners:
        pl.semaphore_signal(barrier, inc=1, device_id=dev, device_id_type=MESH)
    pl.semaphore_wait(barrier, len(partners))

    post(
        x_ref, states.at[y, :, part(core * 8 + hold_x * 2 + hold_z % 2, FB)],
        a1s.at[0], a1r.at[0], holder,
    )

    load_w.wait()

    def lay(i, _):
        block, sub = i // 4, i % 4
        place = (block % 2) * 8 + (block % 8 // 2) * 2 + 1 - block // 8
        rows = part(place * 4 + sub, 32)
        flat = wv[part(i, 32)].reshape(32, 2 * COLS)
        for n in range(GROUPS):
            w[rows, n * 512:n * 512 + 256] = flat[:, n * 256:(n + 1) * 256]
            w[rows, n * 512 + 256:(n + 1) * 512] = flat[:, COLS + n * 256:COLS + (n + 1) * 256]
        return 0

    lax.fori_loop(0, ROWS // 32, lay, 0)
    own = states.at[z // 2, :, part(core * 8 + x * 2 + z % 2, FB)]
    arrived(own, a1s.at[0], a1r.at[0])
    for k in (1, 7, 2, 6, 3, 5, 4):
        post(own, own, a2s.at[k - 1], a2r.at[k - 1], zs[k])
    order = (0, 1, 3, 2)
    for n in order:
        seq = (z // 2 + n) % 4
        for b in range(2):
            other = 2 * seq + b if n else z + 1 - 2 * (z % 2)
            if n or b:
                block = states.at[seq, :, part(core * 8 + x * 2 + other % 2, FB)]
                k = (z + 8 - other) % 8 - 1
                arrived(block, a2s.at[k], a2r.at[k])
        pair = states.at[seq, :, part(core * 4 + x, 2 * FB)]
        for k in (2, 1, 3):
            post(pair, pair, a3s.at[k - 1, n], a3r.at[k - 1, n], xs[k])
    for n in order:
        seq = (z // 2 + n) % 4
        for k in (1, 3, 2):
            pair = states.at[seq, :, part(core * 4 + (x + 4 - k) % 4, 2 * FB)]
            arrived(pair, a3s.at[k - 1, n], a3r.at[k - 1, n])
        half = states.at[seq, :, part(core, HALF)]
        post(half, half, a4s.at[n], a4r.at[n], sibling)
    for n in order:
        half = states.at[(z // 2 + n) % 4, :, part(1 - core, HALF)]
        arrived(half, a4s.at[n], a4r.at[n])
    plus, minus, far = (y + 1) % 4, (y + 3) % 4, (y + 2) % 4

    def project(n):
        acc = dot(
            states[...].reshape(4 * TOK, ROWS), w[:, n * 512:(n + 1) * 512], ((1,), (0,))
        ).reshape(4, TOK, 512)
        for h in range(2):
            kb[n, :, h] = acc[:, :, h * 128:(h + 1) * 128]
            vb[n, :, h] = acc[:, :, 256 + h * 128:256 + (h + 1) * 128].astype(BF)
        for i, (buf, mid, last) in enumerate(((kb, mk, kr), (vb, mv, vr))):
            post(buf.at[n, far, 0], mid.at[n, 0], bs.at[n, i], br.at[n, i], right)
            post(buf.at[n, far, 1], mid.at[n, 1], bs.at[n, 2 + i], br.at[n, 2 + i], left)
            post(buf.at[n, plus, 1], last.at[n, 0, 1], bs.at[n, 4 + i], br.at[n, 4 + i], right)
            post(buf.at[n, minus, 0], last.at[n, 1, 0], bs.at[n, 6 + i], br.at[n, 6 + i], left)

    def merge(n):
        for h, (seq, dev) in enumerate(((plus, right), (minus, left))):
            arrived(mk.at[n, h], bs.at[n, 2 * h], br.at[n, 2 * h])
            fk[n, h] = mk[n, h] + kb[n, seq, h]
            post(fk.at[n, h], kr.at[n, h, h], bs.at[n, 8 + 2 * h], br.at[n, 8 + 2 * h], dev)
            arrived(mv.at[n, h], bs.at[n, 2 * h + 1], br.at[n, 2 * h + 1])
            fv[n, h] = (mv[n, h].astype(F32) + vb[n, seq, h].astype(F32)).astype(BF)
            post(fv.at[n, h], vr.at[n, h, h], bs.at[n, 9 + 2 * h], br.at[n, 9 + 2 * h], dev)

    factor = 1.0 / math.sqrt(HEAD_DIM)

    def one_head(n, h):
        live = lax.broadcasted_iota(jnp.int32, (TOK, DEC), 0) < len_ref[0]
        cols = slice((2 * n + h) * HEAD_DIM, (2 * n + h + 1) * HEAD_DIM)
        keys = kb[n, y, h] + kr[n, 0, h] + kr[n, 1, h]
        values = vb[n, y, h].astype(F32) + vr[n, 0, h].astype(F32) + vr[n, 1, h].astype(F32)
        k1 = keys.astype(BF)
        rest = keys - k1.astype(F32)
        k2 = rest.astype(BF)
        k3 = (rest - k2.astype(F32)).astype(BF)
        v1 = values.astype(BF)
        v2 = (values - v1.astype(F32)).astype(BF)
        qh, gh = q[:, cols], g[:, cols]
        nt, nn, tn = ((1,), (1,)), ((1,), (0,)), ((0,), (0,))
        scores = (dot(k3, qh, nt) + dot(k2, qh, nt) + dot(k1, qh, nt)) * factor
        scores = jnp.where(live, scores, -1e30)
        top = jnp.max(scores, axis=0, keepdims=True)
        expd = jnp.exp(scores - top)
        probs = expd / jnp.sum(expd, axis=0, keepdims=True)
        attn = probs.astype(BF)
        ctx[:, cols] = (dot(attn, v2, tn) + dot(attn, v1, tn)).astype(BF)
        probs_grad = dot(v2, gh, nt) + dot(v1, gh, nt)
        row_dots = jnp.sum(probs * probs_grad, axis=0, keepdims=True)
        score_grad = (probs * (probs_grad - row_dots) * factor).astype(BF)
        lanes = slice(h * HEAD_DIM, (h + 1) * HEAD_DIM)
        kvg[n, 0, 0, :, lanes] = dot(score_grad, qh, nn).astype(BF)
        kvg[n, 0, 1, :, lanes] = dot(attn, gh, nn).astype(BF)

    def attend(n):
        for i, last in enumerate((kr, vr)):
            arrived(last.at[n, 0, 1], bs.at[n, 4 + i], br.at[n, 4 + i])
            arrived(last.at[n, 1, 0], bs.at[n, 6 + i], br.at[n, 6 + i])
            for h in range(2):
                c = 8 + 2 * h + i
                arrived(last.at[n, h, h], bs.at[n, c], br.at[n, c])
        for h in range(2):
            one_head(n, h)
        post(kvg.at[n, 0], kvg.at[n, 3], cs.at[n, 0], cr.at[n, 0], right)
        post(kvg.at[n, 0], kvg.at[n, 1], cs.at[n, 1], cr.at[n, 1], left)

    def pass_on(n):
        arrived(kvg.at[n, 3], cs.at[n, 0], cr.at[n, 0])
        post(kvg.at[n, 3, 0], kvg.at[n, 2, 0], cs.at[n, 2], cr.at[n, 2], right)
        arrived(kvg.at[n, 1], cs.at[n, 1], cr.at[n, 1])
        post(kvg.at[n, 1, 1], kvg.at[n, 2, 1], cs.at[n, 3], cr.at[n, 3], left)

    def far_here(n):
        for h in range(2):
            arrived(kvg.at[n, 2, h], cs.at[n, 2 + h], cr.at[n, 2 + h])

    def early_terms(i, _):
        rows = part(i, 256)
        acc = jnp.zeros((256, 4 * TOK), F32)
        for n in range(2):
            for h in range(2):
                c = (2 * n + h) * 256
                acc += dot(w[rows, c:c + 256], kvg[n, :, h].reshape(4 * TOK, 256), ((1,), (1,)))
        for j in range(4):
            po[j, rows, :] = acc[:, j * TOK:(j + 1) * TOK]
        return 0

    def late_terms(half, j):
        rows = part(half, HALF)
        acc = po[j, rows, :]
        for n in range(2, GROUPS):
            for h in range(2):
                c = (2 * n + h) * 256
                acc += dot(w[rows, c:c + 256], kvg[n, j, h], ((1,), (1,)))
        return acc

    project(0)
    project(1)
    merge(0)
    project(2)
    merge(1)
    project(3)
    load_q.wait()
    load_g.wait()
    attend(0)
    merge(2)
    attend(1)
    merge(3)
    pass_on(0)
    attend(2)
    pass_on(1)
    attend(3)
    save_ctx = pltpu.make_async_copy(ctx, ctx_hbm, in_sem.at[3])
    save_ctx.start()
    pass_on(2)
    far_here(0)
    far_here(1)
    lax.fori_loop(0, ROWS // 256, early_terms, 0)

    def over_cores(j):
        ps[j] = late_terms(1 - core, j).astype(BF)
        post(ps.at[j], pr.at[j], e1s.at[j], e1r.at[j], sibling)
        po[j, part(core, HALF), :] = late_terms(core, j)

    def over_x(j):
        arrived(pr.at[j], e1s.at[j], e1r.at[j])
        both = po[j, part(core, HALF), :] + pr[j].astype(F32)
        po[j, part(core, HALF), :] = both
        s2[j] = both.astype(BF)
        for k in (2, 1, 3):
            post(
                s2.at[j, part((x + k) % 4, 2 * FB)], r2.at[k - 1, j],
                e2s.at[k - 1, j], e2r.at[k - 1, j], xs[k],
            )

    def to_z(j, b):
        to = 2 * ((y + j) % 4) + b
        k = (z + 8 - to) % 8 - 1
        return to != z, remote(
            s3.at[j, b], r3.at[jnp.maximum(k, 0)], e3s.at[2 * j + b],
            e3r.at[jnp.maximum(k, 0)], at(x, y, to, core),
        )

    def over_z(j):
        total = po[j, part(core * 4 + x, 2 * FB), :]
        for k in (1, 3, 2):
            arrived(r2.at[k - 1, j], e2s.at[k - 1, j], e2r.at[k - 1, j])
            total += r2[k - 1, j].astype(F32)
        tot[j] = total.reshape(2, FB, TOK)
        s3[j] = total.reshape(2, FB, TOK).astype(BF)
        for b in range(2):
            away, copy = to_z(j, b)

            @pl.when(away)
            def _():
                copy.start()

            @pl.when(jnp.logical_not(away))
            def _():
                mine[...] = tot[j, b]

    over_cores(0)
    pass_on(3)
    over_cores(3)
    over_x(0)
    over_cores(1)
    over_x(3)
    over_z(0)
    far_here(2)
    far_here(3)
    over_cores(2)
    over_x(1)
    over_z(3)
    over_x(2)
    over_z(1)
    over_z(2)
    total = mine[...]
    for k in range(7):
        arrived(r3.at[k], e3s.at[k], e3r.at[k])
        total += r3[k].astype(F32)
    s4[...] = total.T
    post(s4, r4, e4s.at[0], e4r.at[0], owner)
    arrived(r4, e4s.at[0], e4r.at[0])
    out_ref[...] = r4[...]

    save_ctx.wait()
    for copy in sent:
        copy.wait_send()
    for j in range(4):
        for b in range(2):
            away, copy = to_z(j, b)

            @pl.when(away)
            def _():
                copy.wait_send()


def on_device(enc_states, enc_len, queries, kv_weight, ctx_grad):
    any_spec = pl.BlockSpec(memory_space=pl.ANY)
    vmem = pltpu.VMEM
    dma = lambda *n: pltpu.SemaphoreType.DMA(n)
    context, enc_grad = pl.pallas_call(
        kernel,
        out_shape=(
            jax.ShapeDtypeStruct((DEC, COLS), BF),
            jax.ShapeDtypeStruct((TOK, FB), F32),
        ),
        in_specs=[any_spec, pl.BlockSpec(memory_space=pltpu.SMEM)] + [any_spec] * 3,
        out_specs=(any_spec, pl.BlockSpec(memory_space=pltpu.VMEM)),
        scratch_shapes=[
            vmem((4, TOK, ROWS), BF),
            vmem((ROWS, 2, COLS), BF),
            vmem((ROWS, 2 * COLS), BF),
            vmem((DEC, COLS), BF),
            vmem((DEC, COLS), BF),
            vmem((GROUPS, 4, 2, TOK, HEAD_DIM), F32),
            vmem((GROUPS, 4, 2, TOK, HEAD_DIM), BF),
            vmem((GROUPS, 2, TOK, HEAD_DIM), F32),
            vmem((GROUPS, 2, TOK, HEAD_DIM), BF),
            vmem((GROUPS, 2, TOK, HEAD_DIM), F32),
            vmem((GROUPS, 2, TOK, HEAD_DIM), BF),
            vmem((GROUPS, 2, 2, TOK, HEAD_DIM), F32),
            vmem((GROUPS, 2, 2, TOK, HEAD_DIM), BF),
            vmem((GROUPS, 4, 2, TOK, 2 * HEAD_DIM), BF),
            vmem((DEC, COLS), BF),
            vmem((4, ROWS, TOK), F32),
            vmem((4, HALF, TOK), BF),
            vmem((4, HALF, TOK), BF),
            vmem((4, HALF, TOK), BF),
            vmem((3, 4, 2 * FB, TOK), BF),
            vmem((4, 2, FB, TOK), F32),
            vmem((4, 2, FB, TOK), BF),
            vmem((7, FB, TOK), BF),
            vmem((FB, TOK), F32),
            vmem((TOK, FB), F32),
            vmem((TOK, FB), F32),
            dma(4), dma(1), dma(1), dma(7), dma(7), dma(3, 4), dma(3, 4), dma(4), dma(4),
            dma(GROUPS, 12), dma(GROUPS, 12), dma(GROUPS, 4), dma(GROUPS, 4), dma(4), dma(4),
            dma(3, 4), dma(3, 4), dma(8), dma(7), dma(1), dma(1),
        ],
        compiler_params=pltpu.CompilerParams(
            collective_id=0, has_side_effects=True, vmem_limit_bytes=56 * 2**20
        ),
    )(
        enc_states[0],
        enc_len,
        queries[0, 0],
        kv_weight[0],
        ctx_grad[0, 0],
    )
    return (context[None, None], enc_grad[None])


def solution(mesh):
    return jax.shard_map(
        on_device,
        mesh=mesh,
        in_specs=(
            P("dp", None, ("pipe", "tensor")),
            P("dp"),
            P("pipe", "dp", None, "tensor"),
            P("pipe", "dp", None, "tensor"),
            P("pipe", "dp", None, "tensor"),
        ),
        out_specs=(P("pipe", "dp", None, "tensor"), P("dp", None, ("pipe", "tensor"))),
        check_vma=False,
    )
```

time: 156 us -> 119 us (0.76)
  the two profiles are of different devices: /device:TPU:16 before, /device:TPU:29 now
where the time goes in v2:
time: 119 us
  Pallas kernels  114 us (96%)
  local copies, waits for them, and re-layouts  3.34 us (3%)
  between operations  1.28 us (1%)
    pallas_call x1, Pallas kernels, on_device(): pl.pallas_call(kernel, out_shape=(jax.ShapeDtypeStruct((DEC, COLS), BF),...  114 us
    unnamed x2, local copies, waits for them, and re-layouts  3.34 us

profile of v2, /device:TPU:29, one launch (start us, length us, event | category | flops | bytes accessed | tf_op | source)
XLA Modules:
  0.0 118.5 jit_solution(4281497628801193594)
XLA Ops:
  1.3 113.9 %shard_map.68 = (bf16[256,1024]{1,0:T(8,128)(2,1)}, f32[128,128]{1,0:T(8,128)}) custom-call(bf16[128,128]{1,0:T(8,128)(2,1)} %bitcast.11, s32[1]{0:T(128)S(6)} %copy.9.len_ref, bf16[256,1024]{1,0:T(8,128)(2,1)} %bitcast.7, bf16[2048,2,1024]{2,1,0:T(2,128)(2,1)} %bitcast.6, bf16[256,1024]{1,0:T(8,128)(2,1)} %bitcast.8), custom_call_target="tpu_custom_call" | custom-call | tf_op jit(solution)/shard_map/pallas_call | solution.py:328
  115.2 1.9 %copy.10 = bf16[1,1,256,1024]{3,2,1,0:T(8,128)(2,1)} copy(bf16[1,1,256,1024]{3,2,1,0:T(8,128)(2,1)} %bitcast.9) | data formatting | bytes 1048576
  117.0 1.5 %copy.11 = f32[1,128,128]{2,1,0:T(8,128)} copy(f32[1,128,128]{2,1,0:T(8,128)} %bitcast.10) | data formatting | bytes 131072

commit v3 on v2

--- a/solution.py
+++ b/solution.py
@@ -28,7 +28,7 @@
 def kernel(
     x_ref, len_ref, q_hbm, w_hbm, g_hbm, ctx_hbm, out_ref,
     states, wv, w, q, g, kb, vb, mk, mv, fk, fv, kr, vr, kvg, ctx,
-    po, ps, pr, s2, r2, tot, s3, r3, mine, s4, r4,
+    po, ps, pr, s2, r2, s3, r3, mine, s4, r4,
     in_sem, a1s, a1r, a2s, a2r, a3s, a3r, a4s, a4r,
     bs, br, cs, cr, e1s, e1r, e2s, e2r, e3s, e3r, e4s, e4r,
 ):
@@ -65,9 +65,10 @@
     xs = [at((x + k) % 4, y, z, core) for k in range(4)]
     right, left = at(x, (y + 1) % 4, z, core), at(x, (y + 3) % 4, z, core)
     sibling = at(x, y, z, 1 - core)
-    hold_x, hold_z = zl, 2 * y + 1 - p % 2
+    hold_x, hold_z = (2 * (p // 2 % 2) + 1 - p % 2 + 2 * (zl % 2)) % 4, 2 * y + zl // 2
     holder = at(hold_x, p // 2, hold_z, core)
-    owner = (2 * y + 1 - z % 2, z // 2, x * 2 + core)
+    turn = (x + 4 - 2 * (y % 2)) % 4
+    owner = (2 * y + 1 - turn % 2, z // 2, (z % 2 * 2 + turn // 2) * 2 + core)
 
     load_w = pltpu.make_async_copy(w_hbm, wv, in_sem.at[0])
     load_q = pltpu.make_async_copy(q_hbm, q, in_sem.at[1])
@@ -79,18 +80,13 @@
     partners = zs[1:] + xs[1:] + [right, left, sibling, holder, owner]
     for dev in partners:
         pl.semaphore_signal(barrier, inc=1, device_id=dev, device_id_type=MESH)
-    pl.semaphore_wait(barrier, len(partners))
-
-    post(
-        x_ref, states.at[y, :, part(core * 8 + hold_x * 2 + hold_z % 2, FB)],
-        a1s.at[0], a1r.at[0], holder,
-    )
 
     load_w.wait()
 
     def lay(i, _):
         block, sub = i // 4, i % 4
-        place = (block % 2) * 8 + (block % 8 // 2) * 2 + 1 - block // 8
+        col = (2 * (y % 2) + 1 - block // 8 + 2 * (block // 2 % 2)) % 4
+        place = (block % 2) * 8 + col * 2 + block % 8 // 4
         rows = part(place * 4 + sub, 32)
         flat = wv[part(i, 32)].reshape(32, 2 * COLS)
         for n in range(GROUPS):
@@ -99,63 +95,86 @@
         return 0
 
     lax.fori_loop(0, ROWS // 32, lay, 0)
+    pl.semaphore_wait(barrier, len(partners))
+    post(
+        x_ref, states.at[y, :, part(core * 8 + hold_x * 2 + hold_z % 2, FB)],
+        a1s.at[0], a1r.at[0], holder,
+    )
     own = states.at[z // 2, :, part(core * 8 + x * 2 + z % 2, FB)]
     arrived(own, a1s.at[0], a1r.at[0])
     for k in (1, 7, 2, 6, 3, 5, 4):
         post(own, own, a2s.at[k - 1], a2r.at[k - 1], zs[k])
     order = (0, 1, 3, 2)
+    seqs = [(y + j) % 4 for j in range(4)]
+    step_seq = [(z // 2 + n) % 4 for n in range(4)]
+    step_j = [(z // 2 + n + 4 - y) % 4 for n in range(4)]
     for n in order:
-        seq = (z // 2 + n) % 4
-        for b in range(2):
-            other = 2 * seq + b if n else z + 1 - 2 * (z % 2)
-            if n or b:
-                block = states.at[seq, :, part(core * 8 + x * 2 + other % 2, FB)]
-                k = (z + 8 - other) % 8 - 1
+        for u in range(2):
+            other = 2 * step_seq[n] + u if n else z + 1 - 2 * (z % 2)
+            if n or u:
+                block = states.at[step_seq[n], :, part(core * 8 + x * 2 + other % 2, FB)]
+                k = (z + 7 - other) % 8
                 arrived(block, a2s.at[k], a2r.at[k])
-        pair = states.at[seq, :, part(core * 4 + x, 2 * FB)]
+        pair = states.at[step_seq[n], :, part(core * 4 + x, 2 * FB)]
         for k in (2, 1, 3):
             post(pair, pair, a3s.at[k - 1, n], a3r.at[k - 1, n], xs[k])
-    for n in order:
-        seq = (z // 2 + n) % 4
+
+    def to_sibling(n):
         for k in (1, 3, 2):
-            pair = states.at[seq, :, part(core * 4 + (x + 4 - k) % 4, 2 * FB)]
+            pair = states.at[step_seq[n], :, part(core * 4 + (x + 4 - k) % 4, 2 * FB)]
             arrived(pair, a3s.at[k - 1, n], a3r.at[k - 1, n])
-        half = states.at[seq, :, part(core, HALF)]
+        half = states.at[step_seq[n], :, part(core, HALF)]
         post(half, half, a4s.at[n], a4r.at[n], sibling)
-    for n in order:
-        half = states.at[(z // 2 + n) % 4, :, part(1 - core, HALF)]
-        arrived(half, a4s.at[n], a4r.at[n])
-    plus, minus, far = (y + 1) % 4, (y + 3) % 4, (y + 2) % 4
-
-    def project(n):
-        acc = dot(
-            states[...].reshape(4 * TOK, ROWS), w[:, n * 512:(n + 1) * 512], ((1,), (0,))
-        ).reshape(4, TOK, 512)
+
+    def all_here(n):
+        arrived(states.at[step_seq[n], :, part(1 - core, HALF)], a4s.at[n], a4r.at[n])
+
+    def project(n, step):
+        acc = dot(states[step_seq[step]], w[:, n * 512:(n + 1) * 512], ((1,), (0,)))
         for h in range(2):
-            kb[n, :, h] = acc[:, :, h * 128:(h + 1) * 128]
-            vb[n, :, h] = acc[:, :, 256 + h * 128:256 + (h + 1) * 128].astype(BF)
-        for i, (buf, mid, last) in enumerate(((kb, mk, kr), (vb, mv, vr))):
-            post(buf.at[n, far, 0], mid.at[n, 0], bs.at[n, i], br.at[n, i], right)
-            post(buf.at[n, far, 1], mid.at[n, 1], bs.at[n, 2 + i], br.at[n, 2 + i], left)
-            post(buf.at[n, plus, 1], last.at[n, 0, 1], bs.at[n, 4 + i], br.at[n, 4 + i], right)
-            post(buf.at[n, minus, 0], last.at[n, 1, 0], bs.at[n, 6 + i], br.at[n, 6 + i], left)
-
-    def merge(n):
-        for h, (seq, dev) in enumerate(((plus, right), (minus, left))):
-            arrived(mk.at[n, h], bs.at[n, 2 * h], br.at[n, 2 * h])
-            fk[n, h] = mk[n, h] + kb[n, seq, h]
-            post(fk.at[n, h], kr.at[n, h, h], bs.at[n, 8 + 2 * h], br.at[n, 8 + 2 * h], dev)
-            arrived(mv.at[n, h], bs.at[n, 2 * h + 1], br.at[n, 2 * h + 1])
-            fv[n, h] = (mv[n, h].astype(F32) + vb[n, seq, h].astype(F32)).astype(BF)
-            post(fv.at[n, h], vr.at[n, h, h], bs.at[n, 9 + 2 * h], br.at[n, 9 + 2 * h], dev)
+            kb[n, step_j[step], h] = acc[:, h * 128:(h + 1) * 128]
+            vb[n, step_j[step], h] = acc[:, 256 + h * 128:256 + (h + 1) * 128].astype(BF)
+
+    kinds = ((0, kb, mk, kr), (1, vb, mv, vr))
+
+    def send_far(n):
+        for i, buf, mid, _ in kinds:
+            post(buf.at[n, 2, 0], mid.at[n, 0], bs.at[n, i], br.at[n, i], right)
+            post(buf.at[n, 2, 1], mid.at[n, 1], bs.at[n, 2 + i], br.at[n, 2 + i], left)
+
+    def send_plus(n):
+        for i, buf, _, last in kinds:
+            post(buf.at[n, 1, 1], last.at[n, 0, 1], bs.at[n, 4 + i], br.at[n, 4 + i], right)
+
+    def send_minus(n):
+        for i, buf, _, last in kinds:
+            post(buf.at[n, 3, 0], last.at[n, 1, 0], bs.at[n, 6 + i], br.at[n, 6 + i], left)
+
+    def merge(n, h):
+        j, dev = ((1, right), (3, left))[h]
+        arrived(mk.at[n, h], bs.at[n, 2 * h], br.at[n, 2 * h])
+        fk[n, h] = mk[n, h] + kb[n, j, h]
+        post(fk.at[n, h], kr.at[n, h, h], bs.at[n, 8 + 2 * h], br.at[n, 8 + 2 * h], dev)
+        arrived(mv.at[n, h], bs.at[n, 2 * h + 1], br.at[n, 2 * h + 1])
+        fv[n, h] = (mv[n, h].astype(F32) + vb[n, j, h].astype(F32)).astype(BF)
+        post(fv.at[n, h], vr.at[n, h, h], bs.at[n, 9 + 2 * h], br.at[n, 9 + 2 * h], dev)
+
+    def once(step, j, act):
+        before = len(sent)
+        pl.when(step_j[step] == j)(act)
+        del sent[before:]
+
+    def merges(step, groups):
+        for h, j in enumerate((1, 3)):
+            once(step, j, lambda: [merge(n, h) for n in groups].clear())
 
     factor = 1.0 / math.sqrt(HEAD_DIM)
 
     def one_head(n, h):
         live = lax.broadcasted_iota(jnp.int32, (TOK, DEC), 0) < len_ref[0]
         cols = slice((2 * n + h) * HEAD_DIM, (2 * n + h + 1) * HEAD_DIM)
-        keys = kb[n, y, h] + kr[n, 0, h] + kr[n, 1, h]
-        values = vb[n, y, h].astype(F32) + vr[n, 0, h].astype(F32) + vr[n, 1, h].astype(F32)
+        keys = kb[n, 0, h] + kr[n, 0, h] + kr[n, 1, h]
+        values = vb[n, 0, h].astype(F32) + vr[n, 0, h].astype(F32) + vr[n, 1, h].astype(F32)
         k1 = keys.astype(BF)
         rest = keys - k1.astype(F32)
         k2 = rest.astype(BF)
@@ -201,37 +220,43 @@
             arrived(kvg.at[n, 2, h], cs.at[n, 2 + h], cr.at[n, 2 + h])
 
     def early_terms(i, _):
-        rows = part(i, 256)
-        acc = jnp.zeros((256, 4 * TOK), F32)
-        for n in range(2):
-            for h in range(2):
-                c = (2 * n + h) * 256
-                acc += dot(w[rows, c:c + 256], kvg[n, :, h].reshape(4 * TOK, 256), ((1,), (1,)))
+        rows = part(i, 512)
+        rhs = jnp.concatenate(
+            [kvg[n, :, h].reshape(4 * TOK, 256) for n in range(2) for h in range(2)], axis=1
+        )
+        acc = dot(w[rows, 0:1024], rhs, ((1,), (1,)))
         for j in range(4):
             po[j, rows, :] = acc[:, j * TOK:(j + 1) * TOK]
         return 0
 
-    def late_terms(half, j):
-        rows = part(half, HALF)
-        acc = po[j, rows, :]
-        for n in range(2, GROUPS):
-            for h in range(2):
-                c = (2 * n + h) * 256
-                acc += dot(w[rows, c:c + 256], kvg[n, j, h], ((1,), (1,)))
-        return acc
-
-    project(0)
-    project(1)
-    merge(0)
-    project(2)
-    merge(1)
-    project(3)
+    def late_terms(half, c, size, js):
+        rows = part(half * (HALF // size) + c, size)
+        rhs = jnp.concatenate(
+            [
+                jnp.concatenate([kvg[n, j, h] for j in js], axis=0)
+                for n in range(2, GROUPS) for h in range(2)
+            ],
+            axis=1,
+        )
+        acc = dot(w[rows, 1024:2048], rhs, ((1,), (1,)))
+        return [po[j, rows, :] + acc[:, i * TOK:(i + 1) * TOK] for i, j in enumerate(js)]
+
+    for step in order:
+        to_sibling(step)
+        all_here(step)
+        for n in range(GROUPS):
+            project(n, step)
+            for j, act in ((2, send_far), (1, send_plus), (3, send_minus)):
+                once(step, j, lambda: act(n))
+    for step in order[:3]:
+        merges(step, range(GROUPS))
+    merges(order[3], (0, 1))
     load_q.wait()
     load_g.wait()
     attend(0)
-    merge(2)
+    merges(order[3], (2,))
     attend(1)
-    merge(3)
+    merges(order[3], (3,))
     pass_on(0)
     attend(2)
     pass_on(1)
@@ -241,30 +266,42 @@
     pass_on(2)
     far_here(0)
     far_here(1)
-    lax.fori_loop(0, ROWS // 256, early_terms, 0)
-
-    def over_cores(j):
-        ps[j] = late_terms(1 - core, j).astype(BF)
-        post(ps.at[j], pr.at[j], e1s.at[j], e1r.at[j], sibling)
-        po[j, part(core, HALF), :] = late_terms(core, j)
+    lax.fori_loop(0, ROWS // 512, early_terms, 0)
+
+    def over_cores(js):
+        size = 2 * FB if js == (2,) else HALF
+        parts = [(k, (x + k) % 4) for k in (2, 1, 3, 0)] if js == (2,) else [(0, 0)]
+        for k, c in parts:
+            rows = part(c, size)
+            for j, terms in zip(js, late_terms(1 - core, c, size, js)):
+                ps[j, rows, :] = terms.astype(BF)
+                post(ps.at[j, rows], pr.at[j, rows], e1s.at[j, k], e1r.at[j, k], sibling)
+        for _, c in parts:
+            for j, terms in zip(js, late_terms(core, c, size, js)):
+                po[j, part(core * (HALF // size) + c, size), :] = terms
 
     def over_x(j):
-        arrived(pr.at[j], e1s.at[j], e1r.at[j])
-        both = po[j, part(core, HALF), :] + pr[j].astype(F32)
-        po[j, part(core, HALF), :] = both
-        s2[j] = both.astype(BF)
-        for k in (2, 1, 3):
-            post(
-                s2.at[j, part((x + k) % 4, 2 * FB)], r2.at[k - 1, j],
-                e2s.at[k - 1, j], e2r.at[k - 1, j], xs[k],
-            )
-
-    def to_z(j, b):
-        to = 2 * ((y + j) % 4) + b
-        k = (z + 8 - to) % 8 - 1
+        if j != 2:
+            arrived(pr.at[j], e1s.at[j, 0], e1r.at[j, 0])
+        for k in (2, 1, 3, 0):
+            c = (x + k) % 4
+            rows, own_rows = part(c, 2 * FB), part(core * 4 + c, 2 * FB)
+            if j == 2:
+                arrived(pr.at[j, rows], e1s.at[j, k], e1r.at[j, k])
+            both = po[j, own_rows, :] + pr[j, rows, :].astype(F32)
+            if k:
+                s2[j, k - 1] = both.astype(BF)
+                post(
+                    s2.at[j, k - 1], r2.at[k - 1, j], e2s.at[k - 1, j], e2r.at[k - 1, j], xs[k]
+                )
+            else:
+                po[j, own_rows, :] = both
+
+    def to_z(j, u):
+        to = 2 * seqs[j] + u
+        k = jnp.minimum((z + 7 - to) % 8, 6)
         return to != z, remote(
-            s3.at[j, b], r3.at[jnp.maximum(k, 0)], e3s.at[2 * j + b],
-            e3r.at[jnp.maximum(k, 0)], at(x, y, to, core),
+            s3.at[j, u], r3.at[k], e3s.at[2 * j + u], e3r.at[k], at(x, y, to, core)
         )
 
     def over_z(j):
@@ -272,10 +309,9 @@
         for k in (1, 3, 2):
             arrived(r2.at[k - 1, j], e2s.at[k - 1, j], e2r.at[k - 1, j])
             total += r2[k - 1, j].astype(F32)
-        tot[j] = total.reshape(2, FB, TOK)
         s3[j] = total.reshape(2, FB, TOK).astype(BF)
-        for b in range(2):
-            away, copy = to_z(j, b)
+        for u in range(2):
+            away, copy = to_z(j, u)
 
             @pl.when(away)
             def _():
@@ -283,38 +319,41 @@
 
             @pl.when(jnp.logical_not(away))
             def _():
-                mine[...] = tot[j, b]
-
-    over_cores(0)
+                mine[...] = total[u * FB:(u + 1) * FB]
+
+    over_cores((0,))
     pass_on(3)
-    over_cores(3)
+    over_cores((1, 3))
     over_x(0)
-    over_cores(1)
+    over_x(1)
     over_x(3)
-    over_z(0)
     far_here(2)
     far_here(3)
-    over_cores(2)
-    over_x(1)
+    over_cores((2,))
+    over_z(0)
+    over_z(1)
     over_z(3)
     over_x(2)
-    over_z(1)
     over_z(2)
     total = mine[...]
-    for k in range(7):
+    for k in (0, 6, 1, 5, 2, 4, 3):
         arrived(r3.at[k], e3s.at[k], e3r.at[k])
         total += r3[k].astype(F32)
-    s4[...] = total.T
+    s4[...] = total.T.astype(BF)
     post(s4, r4, e4s.at[0], e4r.at[0], owner)
     arrived(r4, e4s.at[0], e4r.at[0])
-    out_ref[...] = r4[...]
+    out_ref[...] = r4[...].astype(F32)
 
     save_ctx.wait()
     for copy in sent:
         copy.wait_send()
+    for n in range(GROUPS):
+        for i in range(12):
+            buf = (kb, vb)[i % 2].at[n, 0, 0]
+            remote(buf, buf, bs.at[n, i], br.at[n, i], sibling).wait_send()
     for j in range(4):
-        for b in range(2):
-            away, copy = to_z(j, b)
+        for u in range(2):
+            away, copy = to_z(j, u)
 
             @pl.when(away)
             def _():
@@ -352,20 +391,19 @@
             vmem((4, ROWS, TOK), F32),
             vmem((4, HALF, TOK), BF),
             vmem((4, HALF, TOK), BF),
-            vmem((4, HALF, TOK), BF),
+            vmem((4, 3, 2 * FB, TOK), BF),
             vmem((3, 4, 2 * FB, TOK), BF),
-            vmem((4, 2, FB, TOK), F32),
             vmem((4, 2, FB, TOK), BF),
             vmem((7, FB, TOK), BF),
             vmem((FB, TOK), F32),
-            vmem((TOK, FB), F32),
-            vmem((TOK, FB), F32),
+            vmem((TOK, FB), BF),
+            vmem((TOK, FB), BF),
             dma(4), dma(1), dma(1), dma(7), dma(7), dma(3, 4), dma(3, 4), dma(4), dma(4),
-            dma(GROUPS, 12), dma(GROUPS, 12), dma(GROUPS, 4), dma(GROUPS, 4), dma(4), dma(4),
+            dma(GROUPS, 12), dma(GROUPS, 12), dma(GROUPS, 4), dma(GROUPS, 4), dma(4, 4), dma(4, 4),
             dma(3, 4), dma(3, 4), dma(8), dma(7), dma(1), dma(1),
         ],
         compiler_params=pltpu.CompilerParams(
-            collective_id=0, has_side_effects=True, vmem_limit_bytes=56 * 2**20
+            collective_id=0, has_side_effects=True, vmem_limit_bytes=48 * 2**20
         ),
     )(
         enc_states[0],

time: 119 us -> 114 us (0.958)
  the two profiles are of different devices: /device:TPU:29 before, /device:TPU:16 now
where the time goes in v3:
time: 114 us; the launch traced here: 112 us
  Pallas kernels  107 us (94%)
  local copies, waits for them, and re-layouts  4.26 us (4%)
  between operations  1.3 us (1%)
    pallas_call x1, Pallas kernels, on_device(): pl.pallas_call(kernel, out_shape=(jax.ShapeDtypeStruct((DEC, COLS), BF),...  107 us
    unnamed x8, local copies, waits for them, and re-layouts  4.26 us

profile of v3, /device:TPU:16, one launch (start us, length us, event | category | flops | bytes accessed | tf_op | source)
XLA Modules:
  0.0 112.5 jit_solution(3310694414436016672)
XLA Ops:
  1.3 0.0 copy-start
  1.3 1.0 copy-done
  2.3 0.0 copy-start.1
  2.3 1.0 copy-done.1
  3.4 0.0 copy-start.2
  3.4 0.8 copy-done.2
  4.1 106.9 %shard_map.68 = (bf16[256,1024]{1,0:T(8,128)(2,1)S(1)}, f32[128,128]{1,0:T(8,128)S(1)}) custom-call(bf16[128,128]{1,0:T(8,128)(2,1)S(1)} %bitcast.10, s32[1]{0:T(128)S(6)} %copy.9.len_ref, bf16[256,1024]{1,0:T(8,128)(2,1)S(1)} %bitcast.6, bf16[2048,2,1024]{2,1,0:T(2,128)(2,1)} %bitcast.11, bf16[256,1024]{1,0:T(8,128)(2,1)S(1)} %bitcast.7), custom_call_target="tpu_custom_call" | custom-call | tf_op jit(solution)/shard_map/pallas_call | solution.py:367
  111.0 0.8 copy.10
  111.8 0.6 copy.11
Async XLA Ops:
  1.3 1.0 copy-start
  2.3 1.0 copy-start.1
  3.4 0.8 copy-start.2

commit v4 on v3

--- a/solution.py
+++ b/solution.py
@@ -321,19 +321,19 @@
             def _():
                 mine[...] = total[u * FB:(u + 1) * FB]
 
-    over_cores((0,))
     pass_on(3)
     over_cores((1, 3))
-    over_x(0)
+    over_cores((0,))
     over_x(1)
     over_x(3)
+    over_x(0)
     far_here(2)
     far_here(3)
     over_cores((2,))
-    over_z(0)
+    over_x(2)
     over_z(1)
     over_z(3)
-    over_x(2)
+    over_z(0)
     over_z(2)
     total = mine[...]
     for k in (0, 6, 1, 5, 2, 4, 3):

time: 114 us -> 111 us (0.974); the launches traced: 112 us -> 111 us
    pallas_call x1, Pallas kernels: 107 us -> 106 us  [on_device(): pl.pallas_call(kernel, out_shape=(jax.ShapeDtypeStruct((DEC, COLS), BF),...]
where the time goes in v4:
time: 111 us
  Pallas kernels  106 us (95%)
  local copies, waits for them, and re-layouts  4.26 us (4%)
  between operations  1.3 us (1%)
    pallas_call x1, Pallas kernels, on_device(): pl.pallas_call(kernel, out_shape=(jax.ShapeDtypeStruct((DEC, COLS), BF),...  106 us
    unnamed x8, local copies, waits for them, and re-layouts  4.26 us

profile of v4, /device:TPU:16, one launch (start us, length us, event | category | flops | bytes accessed | tf_op | source)
XLA Modules:
  0.0 111.2 jit_solution(13113188438870131146)
XLA Ops:
  1.3 0.0 copy-start
  1.3 1.0 copy-done
  2.3 0.0 copy-start.1
  2.3 1.0 copy-done.1
  3.4 0.0 copy-start.2
  3.4 0.8 copy-done.2
  4.1 105.6 %shard_map.68 = (bf16[256,1024]{1,0:T(8,128)(2,1)S(1)}, f32[128,128]{1,0:T(8,128)S(1)}) custom-call(bf16[128,128]{1,0:T(8,128)(2,1)S(1)} %bitcast.10, s32[1]{0:T(128)S(6)} %copy.9.len_ref, bf16[256,1024]{1,0:T(8,128)(2,1)S(1)} %bitcast.6, bf16[2048,2,1024]{2,1,0:T(2,128)(2,1)} %bitcast.11, bf16[256,1024]{1,0:T(8,128)(2,1)S(1)} %bitcast.7), custom_call_target="tpu_custom_call" | custom-call | tf_op jit(solution)/shard_map/pallas_call | solution.py:367
  109.8 0.8 copy.10
  110.6 0.6 copy.11
Async XLA Ops:
  1.3 1.0 copy-start
  2.3 1.0 copy-start.1
  3.4 0.8 copy-start.2

commit v5 on v4

--- a/solution.py
+++ b/solution.py
@@ -241,14 +241,21 @@
         acc = dot(w[rows, 1024:2048], rhs, ((1,), (1,)))
         return [po[j, rows, :] + acc[:, i * TOK:(i + 1) * TOK] for i, j in enumerate(js)]
 
-    for step in order:
-        to_sibling(step)
-        all_here(step)
+    to_sibling(order[0])
+    all_here(order[0])
+    for i, step in enumerate(order):
         for n in range(GROUPS):
             project(n, step)
             for j, act in ((2, send_far), (1, send_plus), (3, send_minus)):
                 once(step, j, lambda: act(n))
-    for step in order[:3]:
+            if n == 1 and i < 3:
+                to_sibling(order[i + 1])
+        if i == 2:
+            merges(order[0], (0, 1))
+        if i < 3:
+            all_here(order[i + 1])
+    merges(order[0], (2, 3))
+    for step in order[1:3]:
         merges(step, range(GROUPS))
     merges(order[3], (0, 1))
     load_q.wait()
@@ -276,14 +283,16 @@
             for j, terms in zip(js, late_terms(1 - core, c, size, js)):
                 ps[j, rows, :] = terms.astype(BF)
                 post(ps.at[j, rows], pr.at[j, rows], e1s.at[j, k], e1r.at[j, k], sibling)
-        for _, c in parts:
+        for k, c in parts:
             for j, terms in zip(js, late_terms(core, c, size, js)):
                 po[j, part(core * (HALF // size) + c, size), :] = terms
-
-    def over_x(j):
+            if js == (2,):
+                over_x(2, (k,))
+
+    def over_x(j, places=(2, 1, 3, 0)):
         if j != 2:
             arrived(pr.at[j], e1s.at[j, 0], e1r.at[j, 0])
-        for k in (2, 1, 3, 0):
+        for k in places:
             c = (x + k) % 4
             rows, own_rows = part(c, 2 * FB), part(core * 4 + c, 2 * FB)
             if j == 2:
@@ -330,7 +339,6 @@
     far_here(2)
     far_here(3)
     over_cores((2,))
-    over_x(2)
     over_z(1)
     over_z(3)
     over_z(0)

time: 111 us -> 110 us (level)
  Pallas kernels: 106 us -> 104 us
    pallas_call x1, Pallas kernels: 106 us -> 104 us  [on_device(): pl.pallas_call(kernel, out_shape=(jax.ShapeDtypeStruct((DEC, COLS), BF),...]
where the time goes in v5:
time: 110 us; the launch traced here: 109 us
  Pallas kernels  104 us (95%)
  local copies, waits for them, and re-layouts  4.26 us (4%)
  between operations  1.3 us (1%)
    pallas_call x1, Pallas kernels, on_device(): pl.pallas_call(kernel, out_shape=(jax.ShapeDtypeStruct((DEC, COLS), BF),...  104 us
    unnamed x8, local copies, waits for them, and re-layouts  4.26 us

profile of v5, /device:TPU:16, one launch (start us, length us, event | category | flops | bytes accessed | tf_op | source)
XLA Modules:
  0.0 109.3 jit_solution(7133063858932451488)
XLA Ops:
  1.3 0.0 copy-start
  1.3 1.0 copy-done
  2.3 0.0 copy-start.1
  2.3 1.0 copy-done.1
  3.4 0.0 copy-start.2
  3.4 0.8 copy-done.2
  4.1 103.7 %shard_map.68 = (bf16[256,1024]{1,0:T(8,128)(2,1)S(1)}, f32[128,128]{1,0:T(8,128)S(1)}) custom-call(bf16[128,128]{1,0:T(8,128)(2,1)S(1)} %bitcast.10, s32[1]{0:T(128)S(6)} %copy.9.len_ref, bf16[256,1024]{1,0:T(8,128)(2,1)S(1)} %bitcast.6, bf16[2048,2,1024]{2,1,0:T(2,128)(2,1)} %bitcast.11, bf16[256,1024]{1,0:T(8,128)(2,1)S(1)} %bitcast.7), custom_call_target="tpu_custom_call" | custom-call | tf_op jit(solution)/shard_map/pallas_call | solution.py:375
  107.9 0.8 copy.10
  108.6 0.6 copy.11
Async XLA Ops:
  1.3 1.0 copy-start
  2.3 1.0 copy-start.1
  3.4 0.8 copy-start.2

commit v6 on v5

--- a/solution.py
+++ b/solution.py
@@ -250,11 +250,13 @@
                 once(step, j, lambda: act(n))
             if n == 1 and i < 3:
                 to_sibling(order[i + 1])
+            if n == 1 and i == 3:
+                merges(order[0], (2,))
         if i == 2:
             merges(order[0], (0, 1))
         if i < 3:
             all_here(order[i + 1])
-    merges(order[0], (2, 3))
+    merges(order[0], (3,))
     for step in order[1:3]:
         merges(step, range(GROUPS))
     merges(order[3], (0, 1))

time: 110 us -> 110 us (level)
  no operation moved by 1% of the time
where the time goes in v6:
time: 110 us; the launch traced here: 109 us
  Pallas kernels  104 us (95%)
  local copies, waits for them, and re-layouts  4.26 us (4%)
  between operations  1.3 us (1%)
    pallas_call x1, Pallas kernels, on_device(): pl.pallas_call(kernel, out_shape=(jax.ShapeDtypeStruct((DEC, COLS), BF),...  104 us
    unnamed x8, local copies, waits for them, and re-layouts  4.26 us

profile of v6, /device:TPU:16, one launch (start us, length us, event | category | flops | bytes accessed | tf_op | source)
XLA Modules:
  0.0 109.2 jit_solution(3564372127194864853)
XLA Ops:
  1.3 0.0 copy-start
  1.3 1.0 copy-done
  2.3 0.0 copy-start.1
  2.3 1.0 copy-done.1
  3.4 0.0 copy-start.2
  3.4 0.8 copy-done.2
  4.1 103.7 %shard_map.68 = (bf16[256,1024]{1,0:T(8,128)(2,1)S(1)}, f32[128,128]{1,0:T(8,128)S(1)}) custom-call(bf16[128,128]{1,0:T(8,128)(2,1)S(1)} %bitcast.10, s32[1]{0:T(128)S(6)} %copy.9.len_ref, bf16[256,1024]{1,0:T(8,128)(2,1)S(1)} %bitcast.6, bf16[2048,2,1024]{2,1,0:T(2,128)(2,1)} %bitcast.11, bf16[256,1024]{1,0:T(8,128)(2,1)S(1)} %bitcast.7), custom_call_target="tpu_custom_call" | custom-call | tf_op jit(solution)/shard_map/pallas_call | solution.py:377
  107.8 0.8 copy.10
  108.6 0.6 copy.11
Async XLA Ops:
  1.3 1.0 copy-start
  2.3 1.0 copy-start.1
  3.4 0.8 copy-start.2
